TPU v7x, 256 devices: a whole 4x4x8 slice. The times are simulated.
256 devices in a mesh: group: 16 (over z, x_hi), tp: 16 (over x_lo, y, core).
Axes of the slice: x: 4 (x_hi: 2, x_lo: 2; x = x_hi * 2 + x_lo), y: 4, z: 8, core: 2. Of those that a mesh axis runs over, the one named last changes fastest.
Arguments:
- hidden_in: bfloat16 [16, 8, 4, 5120], P('group'), may hold values from -6 to 6
- q_weight: bfloat16 [5120, 4096], P(None, 'tp'), may hold values from -0.078125 to 0.078125
- kv_weight: bfloat16 [5120, 1024], P(None, 'tp'), may hold values from -0.078125 to 0.078125
- o_weight: bfloat16 [4096, 5120], P('tp'), may hold values from -0.09375 to 0.09375
- q_gain: float32 [128], replicated, may hold values from 1 to 8
- k_gain: float32 [128], replicated, may hold values from 1 to 8
- cache: bfloat16 [16, 8, 2, 4, 4096, 128], P('group', None, None, None, 'tp'), may hold values from -6 to 6
- lengths: int32 [16, 8], P('group'), may hold values from 1 to 4092, 16384 in all within a row
- owner: int32 [16], replicated, may hold values from 0 to 15, each once
- a_q: bfloat16 [5120, 64], P('group'), may hold values from -0.078125 to 0.078125
- b_q: bfloat16 [64, 4096], P('group', 'tp'), may hold values from -0.75 to 0.75
- a_o: bfloat16 [4096, 64], P('tp', 'group'), may hold values from -0.09375 to 0.09375
- b_o: bfloat16 [64, 5120], P('group', 'tp'), may hold values from -0.75 to 0.75
Outputs:
- attn_out: bfloat16 [16, 8, 4, 5120], P('group', None, None, 'tp')
Inputs may be any that keep to these rules, and one draw needn't show every extreme that they name: In each group the sequences' lengths sum to 16384 and the largest is 4092. `owner`: a permutation of the group indices.
All inputs are finite; a program needn't handle non-finite values.
Results may differ from a plain program's by a relative error of at most 0.012.
Values may be sent and summed in bfloat16 or wider, within the bound.
No kernel may reach another device: no remote copies, remote signals or barrier semaphores. Data moves between devices by JAX's collectives and lax.ppermute only.
A program may use at most 64 MiB of HBM per device.

v0:
```python
import functools
import math

import jax
import jax.numpy as jnp
from jax import lax
from jax.experimental import pallas as pl
from jax.experimental.pallas import tpu as pltpu
from jax.sharding import PartitionSpec as P

HD = 128
QH = 32
KVH = 4
R = 64
TP = 16
CHIPS = TP // 2
GROUPS = 16
SEQS = 8
STEPS = 4
ROWS = SEQS * STEPS
PER_SEQ = 2 * STEPS
WIDTH = 5120
SLOTS = 256
BLOCK = WIDTH // GROUPS
HALF = BLOCK // 2
OUT = WIDTH // TP
INV_ROOT = 1.0 / math.sqrt(HD)
FAR = -1e30
BF16 = jnp.bfloat16
F32 = jnp.float32

BQ_AT = 80
AO_AT = 88
BO_AT = 96
FACTOR_ROWS = 112
QKV_ROWS = 80
PART_ROWS = 80

VMEM = pl.BlockSpec(memory_space=pltpu.VMEM)
HBM = pl.BlockSpec(memory_space=pltpu.HBM)
ANY = pl.BlockSpec(memory_space=pl.ANY)
SMEM = pl.BlockSpec(memory_space=pltpu.SMEM)
NT = (((1,), (1,)), ((), ()))


def lanes(shape):
    return lax.broadcasted_iota(jnp.int32, shape, len(shape) - 1)


def norm(values, gain):
    mean_square = jnp.mean(values * values, axis=-1, keepdims=True)
    return values * lax.rsqrt(mean_square + 1e-06) * gain


def pack_factors(a_q, b_q, a_o, b_o, out, a_q_in, b_q_in, a_o_in, b_o_in, turned, rows, sems):
    pairs = ((a_q, a_q_in), (b_q, b_q_in), (a_o, a_o_in), (b_o, b_o_in))
    copies = [
        pltpu.make_async_copy(source, place, sems.at[k]) for k, (source, place) in enumerate(pairs)
    ]
    for copy in copies:
        copy.start()
    for copy in copies:
        copy.wait()
    row = lax.broadcasted_iota(jnp.int32, (R, HD), 0)
    unit = jnp.where(lanes((R, HD)) % R == row, 1.0, 0.0).astype(BF16)
    turned[...] = lax.dot_general(
        a_q_in[...], unit, (((0,), (0,)), ((), ())), preferred_element_type=F32
    )
    start = pl.multiple_of((lax.axis_index("tp") % 2) * HALF, HALF)
    first = turned[pl.ds(start, 80), :]
    second = turned[pl.ds(start + 80, 80), :]
    rows[0:80, :] = jnp.where(lanes((80, HD)) < R, first, second)
    bq = b_q_in[...].astype(F32)
    rows[BQ_AT : BQ_AT + 4, :] = bq[:, :HD]
    rows[BQ_AT + 4 : BQ_AT + 8, :] = bq[:, HD:]
    ao = a_o_in[...].astype(F32)
    rows[AO_AT : AO_AT + 4, :] = ao[:, :HD]
    rows[AO_AT + 4 : AO_AT + 8, :] = ao[:, HD:]
    bo = b_o_in[...].astype(F32)
    rows[BO_AT : BO_AT + 4, :] = bo[:, :HD]
    rows[BO_AT + 4 : BO_AT + 8, :] = bo[:, HD : 2 * HD]
    rows[BO_AT + 8 : BO_AT + 16, :] = jnp.zeros((8, HD), F32)
    rows[BO_AT + 8 : BO_AT + 12, 0:64] = bo[:, 2 * HD :]
    message = rows[...].astype(BF16)
    for g in range(GROUPS):
        out[g] = message


def stage_cache(cache, _, out, sems):
    copies = [pltpu.make_async_copy(cache.at[0, s], out.at[0, s], sems.at[s]) for s in range(SEQS)]
    for copy in copies:
        copy.start()
    for copy in copies:
        copy.wait()


def low_rank(owner, tokens, factors, _, __, out, a_true):
    core = lax.axis_index("tp") % 2
    lane = lanes((80, HD))
    left = jnp.where(lane < R, 1.0, 0.0).astype(BF16)
    right = jnp.where(lane < R, 0.0, 1.0).astype(BF16)
    empty = jnp.zeros((HALF, HD), BF16)
    for g in range(GROUPS):
        base = owner[g] * BLOCK
        mine = pl.multiple_of(base + core * HALF, 32)
        other = pl.multiple_of(base + (1 - core) * HALF, 32)
        block = factors[g, 0:80, :]
        a_true[pl.ds(mine, 80), :] = block * left
        a_true[pl.ds(pl.multiple_of(mine + 80, 16), 80), :] = block * right
        a_true[pl.ds(other, HALF), :] = empty
    both = jnp.dot(tokens[...], a_true[...], preferred_element_type=F32)
    out[...] = both + pltpu.roll(both, R, 1)


def unpack_factors(factors, bq_out, ao_out, bo_out, rows):
    for at, pieces, out in ((BQ_AT, 2, bq_out), (AO_AT, 2, ao_out), (BO_AT, 3, bo_out)):
        for g in range(GROUPS):
            block = factors[g, BQ_AT:FACTOR_ROWS, :].astype(F32)
            for h in range(pieces):
                piece = block[at - BQ_AT + 4 * h : at - BQ_AT + 4 * h + 4]
                rows[4 * g : 4 * g + 4, HD * h : HD * h + HD] = piece
        whole = rows[:, : HD * pieces].astype(BF16)
        out[0:R, :] = whole
        out[R : 2 * R, :] = whole


def pack_queries(query_part, kv_own, kv_other, low_own, low_other, bq, gains, out, rows):
    chip, core = lax.axis_index("tp") // 2, lax.axis_index("tp") % 2
    low = low_own[...] + low_other[...]
    lane = lanes((ROWS, HD))
    high = low.astype(BF16).astype(F32)
    low_terms = jnp.where(lane < R, high, low - high).astype(BF16)
    query = query_part[...] + 0.5 * jnp.dot(low_terms, bq[...], preferred_element_type=F32)
    for e in range(2):
        normed = norm(query[:, HD * e : HD * e + HD], gains[0:1, :])
        for s in range(SEQS):
            at = PER_SEQ * s + STEPS * e
            rows[at : at + STEPS, :] = normed[STEPS * s : STEPS * s + STEPS]
    own, other = kv_own[...], kv_other[...]
    left, right = jnp.where(core == 0, own, other), jnp.where(core == 0, other, own)
    head = jnp.concatenate([left, right], axis=1)
    head = jnp.where(chip < KVH, norm(head, gains[1:2, :]), head)
    rows[64:80, :] = jnp.where(core == 0, head[0:16], head[16:32])
    message = rows[...].astype(BF16)
    for i in range(CHIPS):
        out[i] = message


def cached_attention(
    lengths, mine, theirs, cache, own_part, other_part, queries, weighted, scores, weights
):
    first = lax.axis_index("tp") * SLOTS
    core = lax.axis_index("tp") % 2
    for i in range(CHIPS):
        queries[2 * i + core] = mine[i, 0:64, :].astype(F32)
        queries[2 * i + 1 - core] = theirs[i, 0:64, :].astype(F32)
    position = lanes((HD, SLOTS)) + first
    lane = lanes((HD, HD))
    for s in range(SEQS):
        query = queries[:, PER_SEQ * s : PER_SEQ * s + PER_SEQ, :].reshape(HD, HD).astype(BF16)
        for c in range(KVH):
            scores[s, ROWS * c : ROWS * c + ROWS, :] = lax.dot_general(
                query[ROWS * c : ROWS * c + ROWS],
                cache[0, s, 0, c],
                NT,
                preferred_element_type=F32,
            )
    logs = jnp.zeros((HD, HD), F32)
    inverse = []
    for s in range(SEQS):
        score = jnp.where(position < lengths[0, s], scores[s] * INV_ROOT, FAR)
        largest = score.max(axis=-1, keepdims=True)
        weight = jnp.exp(score - largest)
        total = weight.sum(axis=-1, keepdims=True)
        weights[s] = weight.astype(BF16)
        log = jnp.where(largest > 0.5 * FAR, largest + jnp.log(total), FAR)
        logs = jnp.where(lane % SEQS == s, log, logs)
        inverse.append(1.0 / total)
    for s in range(SEQS):
        value = [
            jnp.dot(
                weights[s, ROWS * c : ROWS * c + ROWS, :],
                cache[0, s, 1, c],
                preferred_element_type=F32,
            )
            for c in range(KVH)
        ]
        value = jnp.concatenate(value, axis=0) * inverse[s]
        weighted[:, PER_SEQ * s : PER_SEQ * s + PER_SEQ, :] = value.reshape(TP, PER_SEQ, HD)
    high = logs.astype(BF16).astype(F32)
    middle = (logs - high).astype(BF16).astype(F32)
    terms = jnp.where(lane < 8, high, jnp.where(lane < 16, middle, logs - high - middle))
    weighted[:, 64:72, :] = terms.reshape(TP, PER_SEQ, HD)
    weighted[:, 72:80, :] = jnp.zeros((TP, 8, HD), F32)
    for i in range(CHIPS):
        own_part[i] = weighted[2 * i + core]
        other_part[i] = weighted[2 * i + 1 - core].astype(BF16)


def log_sum(terms):
    return terms + pltpu.roll(terms, HD - 8, 1) + pltpu.roll(terms, HD - 16, 1)


def spread(shares):
    rows = shares.shape[0]
    high = shares.astype(BF16).astype(F32)
    low = pltpu.roll(shares - high, SEQS, 1)
    terms = jnp.where(lanes((rows, HD)) < SEQS, high, low).astype(BF16)[:, : 2 * SEQS]
    row = lax.broadcasted_iota(jnp.int32, (2 * SEQS, SEQS * HD), 0)
    unit = jnp.where(row % SEQS == lanes((2 * SEQS, SEQS * HD)) // HD, 1.0, 0.0).astype(BF16)
    return jnp.dot(terms, unit, preferred_element_type=F32)


def merge_parts(own, other, _, out):
    lane = lanes((64, HD))
    theirs = [other[i].astype(F32) for i in range(CHIPS)]
    logs = [
        log_sum(jnp.concatenate([own[i, 64:72, :] for i in range(CHIPS)], axis=0)),
        log_sum(jnp.concatenate([part[64:72] for part in theirs], axis=0)),
    ]
    largest = jnp.maximum(logs[0], logs[1])
    shares = [jnp.exp(log - largest) for log in logs]
    total = shares[0] + shares[1]
    inverse = 1.0 / total
    wide = spread(jnp.concatenate([shares[0] * inverse, shares[1] * inverse], axis=0))
    log = largest + jnp.log(total)
    high = log.astype(BF16).astype(F32)
    middle = (log - high).astype(BF16).astype(F32)
    low = log - high - middle
    terms = jnp.where(lane < 16, pltpu.roll(middle, 8, 1), pltpu.roll(low, 16, 1))
    terms = jnp.where(lane < 8, high, terms)
    for i in range(CHIPS):
        at = PER_SEQ * i
        rows = []
        for s in range(SEQS):
            block = slice(HD * s, HD * s + HD)
            rows.append(
                own[i, PER_SEQ * s : PER_SEQ * s + PER_SEQ, :] * wide[at : at + PER_SEQ, block]
                + theirs[i][PER_SEQ * s : PER_SEQ * s + PER_SEQ]
                * wide[64 + at : 64 + at + PER_SEQ, block]
            )
        rows.append(terms[at : at + PER_SEQ])
        rows.append(jnp.zeros((PER_SEQ, HD), F32))
        out[i] = jnp.concatenate(rows, axis=0).astype(BF16)


def fresh_attention(mine, theirs, out, logs):
    chip, core = lax.axis_index("tp") // 2, lax.axis_index("tp") % 2
    head = chip // (CHIPS // KVH)

    def whole(at):
        own, other = mine[at, 64:80, :].astype(F32), theirs[at, 64:80, :].astype(F32)
        low, high = jnp.where(core == 0, own, other), jnp.where(core == 0, other, own)
        return jnp.concatenate([low, high], axis=0).astype(BF16)

    keys, values = whole(head), whole(KVH + head)
    scores = (
        lax.dot_general(mine[chip, 0:64, :], keys, NT, preferred_element_type=F32) * INV_ROOT
    )
    row = lax.broadcasted_iota(jnp.int32, (64, ROWS), 0)
    column = lanes((64, ROWS))
    seen = (row // PER_SEQ == column // STEPS) & (row % STEPS >= column % STEPS)
    scores = jnp.where(seen, scores, FAR)
    largest = scores.max(axis=-1, keepdims=True)
    weights = jnp.where(seen, jnp.exp(scores - largest), 0.0)
    total = weights.sum(axis=-1, keepdims=True)
    value = jnp.dot(weights.astype(BF16), values, preferred_element_type=F32)
    out[...] = value / total
    log = largest + jnp.log(total)
    lane = lanes((PER_SEQ, HD))
    compact = jnp.zeros((PER_SEQ, HD), F32)
    for s in range(SEQS):
        compact = jnp.where(lane == s, log[PER_SEQ * s : PER_SEQ * s + PER_SEQ], compact)
    logs[...] = compact


def place_columns(heads, low, o_in, core, out):
    lane = lanes((ROWS, HD))
    for k in range(CHIPS):
        start = pl.multiple_of(2 * OUT * k + 2 * HD * core, HD)
        value = jnp.dot(heads, o_in[:, pl.ds(start, 3 * HD)], preferred_element_type=F32)
        first, last = value[:, :HD], value[:, 2 * HD :]
        first = jnp.where((lane < R) & (core == 1), low, first)
        last = jnp.where((lane >= R) & (core == 0), low, last)
        out[k, :, 0:HD] = first.astype(out.dtype)
        out[k, :, HD : 2 * HD] = value[:, HD : 2 * HD].astype(out.dtype)
        out[k, :, 2 * HD :] = last.astype(out.dtype)


def project_theirs(
    received, fresh, fresh_logs, ao, o_in, theirs, heads, low, attended
):
    logs = []
    for i in range(CHIPS):
        logs.append(log_sum(received[i, 64:80, :].astype(F32)[0:8]))
    logs.append(fresh_logs[...])
    largest = functools.reduce(jnp.maximum, logs)
    shares = [jnp.exp(log - largest) for log in logs]
    inverse = 1.0 / functools.reduce(jnp.add, shares)
    wide = spread(jnp.concatenate([share * inverse for share in shares], axis=0))
    for pair in range(SEQS // 2):
        blocks = [received[i, 16 * pair : 16 * pair + 16, :].astype(F32) for i in range(CHIPS)]
        for s in (2 * pair, 2 * pair + 1):
            at, block = PER_SEQ * s, slice(HD * s, HD * s + HD)
            total = fresh[at : at + PER_SEQ, :] * wide[64:72, block]
            for i in range(CHIPS):
                part = blocks[i][at - 16 * pair : at - 16 * pair + PER_SEQ]
                total = total + part * wide[PER_SEQ * i : PER_SEQ * i + PER_SEQ, block]
            for e in range(2):
                attended[STEPS * s : STEPS * s + STEPS, HD * e : HD * e + HD] = total[
                    STEPS * e : STEPS * e + STEPS
                ]
    heads[...] = attended[...].astype(BF16)
    low[...] = lax.dot_general(heads[...], ao[...], NT, preferred_element_type=F32)
    place_columns(heads[...], low[...], o_in, 1 - lax.axis_index("tp") % 2, theirs)


def project_mine(heads, low, o_in, mine):
    place_columns(heads[...], low[...], o_in, lax.axis_index("tp") % 2, mine)


def add_pair(mine, theirs, out):
    for k in range(CHIPS):
        out[k] = (mine[k] + theirs[k].astype(F32)).astype(BF16)


def finish(received, bo, out):
    odd = lax.axis_index("tp") % 2 == 1
    total = received[0].astype(F32)
    for i in range(1, CHIPS):
        total = total + received[i].astype(F32)
    lane = lanes((ROWS, HD))
    low = jnp.where(
        odd,
        jnp.where(lane < R, total[:, :HD], 0.0),
        jnp.where(lane < R, 0.0, total[:, 2 * HD :]),
    )
    high = low.astype(BF16)
    rest = (low - high.astype(F32)).astype(BF16)
    extra = jnp.dot(high, bo[...], preferred_element_type=F32) + jnp.dot(
        rest, bo[...], preferred_element_type=F32
    )
    moved = pltpu.roll(total, 3 * HD - R, 1)
    result = (jnp.where(odd, moved, total) + 0.5 * extra)[:, :OUT].astype(BF16)
    for s in range(SEQS):
        out[0, s] = result[STEPS * s : STEPS * s + STEPS]


def call(kernel, in_specs, outs, scratch=(), vmem=24):
    single = not isinstance(outs, (list, tuple))
    return pl.pallas_call(
        kernel,
        out_shape=outs,
        in_specs=in_specs,
        out_specs=VMEM if single else [VMEM] * len(outs),
        scratch_shapes=list(scratch),
        cost_estimate=pl.CostEstimate(flops=1_000_000, bytes_accessed=1_000_000, transcendentals=0),
        compiler_params=pltpu.CompilerParams(vmem_limit_bytes=vmem * 1024 * 1024),
    )


def shape(*dims, dtype=BF16):
    return jax.ShapeDtypeStruct(dims, dtype)


def per_device(
    hidden_in,
    q_weight,
    kv_weight,
    o_weight,
    q_gain,
    k_gain,
    cache,
    lengths,
    owner,
    a_q,
    b_q,
    a_o,
    b_o,
):
    tokens = hidden_in.reshape(ROWS, WIDTH)
    other_core = [(i, i ^ 1) for i in range(TP)]
    same_core = [list(range(0, TP, 2)), list(range(1, TP, 2))]
    q_gain, k_gain = q_gain.reshape(1, HD), k_gain.reshape(1, HD)

    message = call(
        pack_factors,
        [HBM] * 4,
        shape(GROUPS, FACTOR_ROWS, HD),
        [
            pltpu.VMEM((R, BLOCK), BF16),
            pltpu.VMEM((4, 2 * HD), BF16),
            pltpu.VMEM((4, 2 * HD), BF16),
            pltpu.VMEM((4, OUT), BF16),
            pltpu.VMEM((BLOCK, HD), F32),
            pltpu.VMEM((FACTOR_ROWS, HD), F32),
            pltpu.SemaphoreType.DMA((4,)),
        ],
        vmem=60,
    )(a_q.T, b_q, a_o.T, b_o)
    factors = lax.all_to_all(message, "group", 0, 0)

    query_part = jnp.dot(tokens, q_weight, preferred_element_type=F32)
    keyval_part = jnp.dot(tokens, kv_weight, preferred_element_type=F32)

    gains = jnp.concatenate([q_gain, k_gain], axis=0)
    kv_other = lax.ppermute(keyval_part, "tp", other_core)
    low_own = call(
        low_rank,
        [SMEM, VMEM, VMEM, VMEM, VMEM],
        shape(ROWS, HD, dtype=F32),
        [pltpu.VMEM((WIDTH, HD), BF16)],
    )(owner, tokens, factors, kv_other, gains)
    low_other = lax.ppermute(low_own, "tp", other_core)
    bq, ao, bo = call(
        unpack_factors,
        [VMEM],
        [shape(2 * R, 2 * HD), shape(2 * R, 2 * HD), shape(2 * R, 3 * HD)],
        [pltpu.VMEM((R, 3 * HD), F32)],
    )(factors)
    message = call(
        pack_queries,
        [VMEM] * 7,
        shape(CHIPS, QKV_ROWS, HD),
        [pltpu.VMEM((QKV_ROWS, HD), F32)],
    )(query_part, keyval_part, kv_other, low_own, low_other, bq, gains)
    mine = lax.all_to_all(message, "tp", 0, 0, axis_index_groups=same_core)
    cache = call(
        stage_cache,
        [ANY, ANY],
        shape(*cache.shape),
        [pltpu.SemaphoreType.DMA((SEQS,))],
    )(cache, message)
    theirs = lax.ppermute(mine, "tp", other_core)

    own_part, other_part = call(
        cached_attention,
        [SMEM, VMEM, VMEM, VMEM],
        [shape(CHIPS, PART_ROWS, HD, dtype=F32), shape(CHIPS, PART_ROWS, HD)],
        [
            pltpu.VMEM((TP, 64, HD), F32),
            pltpu.VMEM((TP, PART_ROWS, HD), F32),
            pltpu.VMEM((SEQS, HD, SLOTS), F32),
            pltpu.VMEM((SEQS, HD, SLOTS), BF16),
        ],
    )(lengths, mine, theirs, cache)
    other_part = lax.ppermute(other_part, "tp", other_core)
    fresh, fresh_logs = call(
        fresh_attention,
        [VMEM] * 2,
        [shape(64, HD, dtype=F32), shape(PER_SEQ, HD, dtype=F32)],
    )(mine, theirs)

    message = call(merge_parts, [VMEM] * 3, shape(CHIPS, PART_ROWS, HD))(
        own_part, other_part, fresh_logs
    )
    parts = lax.all_to_all(message, "tp", 0, 0, axis_index_groups=same_core)
    theirs, heads, low = call(
        project_theirs,
        [VMEM] * 5,
        [shape(CHIPS, ROWS, 3 * HD), shape(ROWS, 2 * HD), shape(ROWS, HD, dtype=F32)],
        [pltpu.VMEM((ROWS, 2 * HD), F32)],
    )(parts, fresh, fresh_logs, ao, o_weight)
    theirs = lax.ppermute(theirs, "tp", other_core)
    mine = call(
        project_mine,
        [VMEM] * 3,
        shape(CHIPS, ROWS, 3 * HD, dtype=F32),
    )(heads, low, o_weight)
    message = call(add_pair, [VMEM, VMEM], shape(CHIPS, ROWS, 3 * HD))(mine, theirs)
    sums = lax.all_to_all(message, "tp", 0, 0, axis_index_groups=same_core)
    return call(finish, [VMEM, VMEM], shape(1, SEQS, STEPS, OUT))(sums, bo)


def solution(mesh):
    placed = (
        P("group", None, None, None),
        P(None, "tp"),
        P(None, "tp"),
        P("tp", None),
        P(),
        P(),
        P("group", None, None, None, "tp", None),
        P("group", None),
        P(),
        P("group", None),
        P("group", "tp"),
        P("tp", "group"),
        P("group", "tp"),
    )
    return jax.shard_map(
        per_device,
        mesh=mesh,
        in_specs=placed,
        out_specs=P("group", None, None, "tp"),
        check_vma=False,
    )
```

profile of v0, /device:TPU:1, one launch (start us, length us, event | category | flops | bytes accessed | tf_op | source)
XLA Modules:
  0.0 70.8 jit_solution(4412184658379810537)
XLA Ops:
  0.0 0.0 copy-start
  0.0 0.0 copy-start.4
  0.0 2.0 %shard_map.127 = bf16[16,112,128]{2,1,0:T(8,128)(2,1)} custom-call(bf16[64,320]{1,0:T(8,128)(2,1)} %bitcast.8, bf16[4,256]{1,0:T(4,128)(2,1)} %b_q.1, bf16[4,256]{1,0:T(4,128)(2,1)} %bitcast.9, bf16[4,320]{1,0:T(4,128)(2,1)} %b_o.1), custom_call_target="tpu_custom_call" | custom-call | flops 1000000 | bytes 1000000 | tf_op jit(solution)/shard_map/pallas_call | solution.py:386
  2.0 11.6 %all-to-all-start = ((bf16[16,112,128]{2,1,0:T(8,128)(2,1)}), bf16[16,112,128]{2,1,0:T(8,128)(2,1)S(1)}, u32[]{:S(2)}, u32[]{:S(2)}) async-start(bf16[16,112,128]{2,1,0:T(8,128)(2,1)} %shard_map.127), calls=%async_computation | async-start | bytes 917504 | tf_op jit(solution)/shard_map/all_to_all | solution.py:401
  13.6 1.1 %reshape.9.tokens = bf16[32,5120]{1,0:T(8,128)(2,1)S(1)} reshape(bf16[1,8,4,5120]{3,2,1,0:T(4,128)(2,1)} %param.13) | data formatting | bytes 655360 | tf_op jit(solution)/shard_map/reshape | solution.py:381
  14.7 1.4 %fusion.1.kv_own = f32[32,64]{1,0:T(8,128)S(1)} fusion(bf16[32,5120]{1,0:T(8,128)(2,1)S(1)} %reshape.9.tokens, bf16[5120,64]{0,1:T(8,128)(2,1)} %param.15), kind=kOutput, calls=%fused_computation.2 | convolution fusion | flops 20971520 | bytes 991232 | tf_op jit(solution)/shard_map/dot_general | solution.py:404
  16.1 1.0 %collective-permute-start = (f32[32,64]{1,0:T(8,128)S(1)}, f32[32,64]{1,0:T(8,128)S(1)}, u32[]{:S(2)}, u32[]{:S(2)}) collective-permute-start(f32[32,64]{1,0:T(8,128)S(1)} %fusion.1.kv_own), channel_id=1, source_target_pairs={{0,1},{1,0},{2,3},{3,2},{4,5},{5,4},{6,7},{7,6},{8,9},{9,8},{10,11... | collective-permute-start | bytes 24584 | tf_op jit(solution)/shard_map/ppermute | solution.py:407
  17.0 0.8 %collective-permute-done._.kv_other = f32[32,64]{1,0:T(8,128)S(1)} collective-permute-done((f32[32,64]{1,0:T(8,128)S(1)}, f32[32,64]{1,0:T(8,128)S(1)}, u32[]{:S(2)}, u32[]{:S(2)}) %collective-permute-start) | collective-permute-done | bytes 8224 | tf_op jit(solution)/shard_map/ppermute | solution.py:407
  17.9 11.8 %all-to-all-done.factors = bf16[16,112,128]{2,1,0:T(8,128)(2,1)S(1)} async-done(((bf16[16,112,128]{2,1,0:T(8,128)(2,1)}), bf16[16,112,128]{2,1,0:T(8,128)(2,1)S(1)}, u32[]{:S(2)}, u32[]{:S(2)}) %all-to-all-start) | async-done | bytes 458784 | tf_op jit(solution)/shard_map/all_to_all | solution.py:401
  29.6 1.1 %shard_map.128.low_own = f32[32,128]{1,0:T(8,128)S(1)} custom-call(s32[16]{0:T(128)S(1)} %copy-done.4, bf16[32,5120]{1,0:T(8,128)(2,1)S(1)} %reshape.9.tokens, bf16[16,112,128]{2,1,0:T(8,128)(2,1)S(1)} %all-to-all-done.factors, f32[32,64]{1,0:T(8,128)S(1)} %collective-permute-done._.kv_other, f32[2,128]{1,0:T(2,128)S(1)} %pad_maximum_fusion.__.gains), custom_call_target="tpu_custom_call" | custom-call | flops 1000000 | bytes 1000000 | tf_op jit(solution)/shard_map/pallas_call | solution.py:408
  30.7 2.3 %collective-permute-start.1 = (f32[32,128]{1,0:T(8,128)S(1)}, f32[32,128]{1,0:T(8,128)S(1)}, u32[]{:S(2)}, u32[]{:S(2)}) collective-permute-start(f32[32,128]{1,0:T(8,128)S(1)} %shard_map.128.low_own), channel_id=1, source_target_pairs={{0,1},{1,0},{2,3},{3,2},{4,5},{5,4},{6,7},{7,6},{8,9},{9,8},{10,11... | collective-permute-start | bytes 49160 | tf_op jit(solution)/shard_map/ppermute | solution.py:414
  33.0 0.6 fusion.query_part
  33.6 0.1 shard_map.129
  33.7 0.2 collective-permute-done.1.low_other
  33.9 0.2 shard_map.130._
  34.1 9.8 %all_to_all.20.mine = bf16[8,80,128]{2,1,0:T(8,128)(2,1)S(1)} all-to-all(bf16[8,80,128]{2,1,0:T(8,128)(2,1)S(1)} %shard_map.130._), channel_id=1, replica_groups={{0,2,4,6,8,10,12,14},{1,3,5,7,9,11,13,15},{16,18,20,22,24,26,28,30},{17..., dimensions={0} | all-to-all | bytes 327680 | tf_op jit(solution)/shard_map/all_to_all | solution.py:427
  43.9 1.6 %collective-permute-start.2 = (bf16[8,80,128]{2,1,0:T(8,128)(2,1)S(1)}, bf16[8,80,128]{2,1,0:T(8,128)(2,1)S(1)}, u32[]{:S(2)}, u32[]{:S(2)}) collective-permute-start(bf16[8,80,128]{2,1,0:T(8,128)(2,1)S(1)} %all_to_all.20.mine), channel_id=1, source_target_pairs={{0,1},{1,0},{2,3},{3,2},{4,5},{5,4},{6,7},{7,6},{8,9},{9,8},{10,11... | collective-permute-start | bytes 491528 | tf_op jit(solution)/shard_map/ppermute | solution.py:434
  45.5 0.4 shard_map.131.cache
  45.9 0.0 copy-start.1
  45.9 0.6 collective-permute-done.2.theirs
  46.6 1.8 %shard_map.132 = (f32[8,80,128]{2,1,0:T(8,128)S(1)}, bf16[8,80,128]{2,1,0:T(8,128)(2,1)S(1)}) custom-call(s32[1,8]{1,0:T(1,128)S(1)} %copy-done.3, bf16[8,80,128]{2,1,0:T(8,128)(2,1)S(1)} %all_to_all.20.mine, bf16[8,80,128]{2,1,0:T(8,128)(2,1)S(1)} %collective-permute-done.2.theirs, bf16[1,8,2,4,256,128]{5,4,3,2,1,0:T(8,128)(2,1)S(1)} %shard_map.131.cache), custom_call_target="tpu_custom_call" | custom-call | flops 1000000 | bytes 1000000 | tf_op jit(solution)/shard_map/pallas_call | solution.py:436
  48.4 0.5 collective-permute-start.3
  48.8 0.3 shard_map.133
  49.2 0.7 collective-permute-done.3.other
  49.9 0.4 shard_map.134
  50.2 8.1 %all_to_all.21.received = bf16[8,80,128]{2,1,0:T(8,128)(2,1)S(1)} all-to-all(bf16[8,80,128]{2,1,0:T(8,128)(2,1)S(1)} %shard_map.134), channel_id=1, replica_groups={{0,2,4,6,8,10,12,14},{1,3,5,7,9,11,13,15},{16,18,20,22,24,26,28,30},{17..., dimensions={0} | all-to-all | bytes 327680 | tf_op jit(solution)/shard_map/all_to_all | solution.py:457
  58.4 0.7 shard_map.135
  59.1 1.6 %collective-permute-start.4 = (bf16[8,32,384]{2,1,0:T(8,128)(2,1)S(1)}, bf16[8,32,384]{2,1,0:T(8,128)(2,1)S(1)}, u32[]{:S(2)}, u32[]{:S(2)}) collective-permute-start(bf16[8,32,384]{2,1,0:T(8,128)(2,1)S(1)} %get-tuple-element.23), channel_id=1, source_target_pairs={{0,1},{1,0},{2,3},{3,2},{4,5},{5,4},{6,7},{7,6},{8,9},{9,8},{10,11... | collective-permute-start | bytes 589832 | tf_op jit(solution)/shard_map/ppermute | solution.py:464
  60.7 0.3 shard_map.136.mine
  61.0 0.7 %collective-permute-done.4.theirs = bf16[8,32,384]{2,1,0:T(8,128)(2,1)S(1)} collective-permute-done((bf16[8,32,384]{2,1,0:T(8,128)(2,1)S(1)}, bf16[8,32,384]{2,1,0:T(8,128)(2,1)S(1)}, u32[]{:S(2)}, u32[]{:S(2)}) %collective-permute-start.4) | collective-permute-done | bytes 196640 | tf_op jit(solution)/shard_map/ppermute | solution.py:464
  61.8 8.3 %all_to_all.22.received = bf16[8,32,384]{2,1,0:T(8,128)(2,1)S(1)} all-to-all(bf16[8,32,384]{2,1,0:T(8,128)(2,1)S(1)} %shard_map.137), channel_id=1, replica_groups={{0,2,4,6,8,10,12,14},{1,3,5,7,9,11,13,15},{16,18,20,22,24,26,28,30},{17..., dimensions={0} | all-to-all | bytes 393216 | tf_op jit(solution)/shard_map/all_to_all | solution.py:471
  70.1 0.8 %shard_map.138 = bf16[1,8,4,320]{3,2,1,0:T(4,128)(2,1)} custom-call(bf16[8,32,384]{2,1,0:T(8,128)(2,1)S(1)} %all_to_all.22.received, bf16[128,384]{1,0:T(8,128)(2,1)S(1)} %get-tuple-element.24.bo), custom_call_target="tpu_custom_call" | custom-call | flops 1000000 | bytes 1000000 | tf_op jit(solution)/shard_map/pallas_call | solution.py:472
  (13 shorter events, 0.1 us)
Async XLA Ops:
  0.0 33.0 %copy-start = (bf16[5120,256]{1,0:T(8,128)(2,1)S(1)}, bf16[5120,256]{1,0:T(8,128)(2,1)}, u32[]{:S(2)}) copy-start(bf16[5120,256]{1,0:T(8,128)(2,1)} %param.14) | copy-start | bytes 7864324
  0.0 17.0 %copy-start.6 = (f32[128]{0:T(128)S(1)}, f32[128]{0:T(128)}, u32[]{:S(2)}) copy-start(f32[128]{0:T(128)} %param.17) | copy-start | bytes 1540
  0.0 17.0 %copy-start.5 = (f32[128]{0:T(128)S(1)}, f32[128]{0:T(128)}, u32[]{:S(2)}) copy-start(f32[128]{0:T(128)} %param.18) | copy-start | bytes 1540
  0.0 29.6 %copy-start.4 = (s32[16]{0:T(128)S(1)}, s32[16]{0:T(128)}, u32[]{:S(2)}) copy-start(s32[16]{0:T(128)} %owner.1) | copy-start | bytes 196
  2.0 27.6 %all-to-all-start = ((bf16[16,112,128]{2,1,0:T(8,128)(2,1)}), bf16[16,112,128]{2,1,0:T(8,128)(2,1)S(1)}, u32[]{:S(2)}, u32[]{:S(2)}) async-start(bf16[16,112,128]{2,1,0:T(8,128)(2,1)} %shard_map.127), calls=%async_computation | async-start | bytes 917504 | tf_op jit(solution)/shard_map/all_to_all | solution.py:401
  16.1 1.8 %collective-permute-start = (f32[32,64]{1,0:T(8,128)S(1)}, f32[32,64]{1,0:T(8,128)S(1)}, u32[]{:S(2)}, u32[]{:S(2)}) collective-permute-start(f32[32,64]{1,0:T(8,128)S(1)} %fusion.1.kv_own), channel_id=1, source_target_pairs={{0,1},{1,0},{2,3},{3,2},{4,5},{5,4},{6,7},{7,6},{8,9},{9,8},{10,11... | collective-permute-start | bytes 24584 | tf_op jit(solution)/shard_map/ppermute | solution.py:407
  29.6 15.9 %copy-start.2 = (bf16[1,8,2,4,256,128]{5,4,3,2,1,0:T(8,128)(2,1)S(1)}, bf16[1,8,2,4,256,128]{5,4,3,2,1,0:T(8,128)(2,1)}, u32[]{:S(2)}) copy-start(bf16[1,8,2,4,256,128]{5,4,3,2,1,0:T(8,128)(2,1)} %cache.1) | copy-start | bytes 12582916
  30.7 3.2 %collective-permute-start.1 = (f32[32,128]{1,0:T(8,128)S(1)}, f32[32,128]{1,0:T(8,128)S(1)}, u32[]{:S(2)}, u32[]{:S(2)}) collective-permute-start(f32[32,128]{1,0:T(8,128)S(1)} %shard_map.128.low_own), channel_id=1, source_target_pairs={{0,1},{1,0},{2,3},{3,2},{4,5},{5,4},{6,7},{7,6},{8,9},{9,8},{10,11... | collective-permute-start | bytes 49160 | tf_op jit(solution)/shard_map/ppermute | solution.py:414
  43.9 2.7 %copy-start.3 = (s32[1,8]{1,0:T(1,128)S(1)}, s32[1,8]{1,0:T(1,128)}, u32[]{:S(2)}) copy-start(s32[1,8]{1,0:T(1,128)} %lengths.1) | copy-start | bytes 100
  43.9 2.7 %collective-permute-start.2 = (bf16[8,80,128]{2,1,0:T(8,128)(2,1)S(1)}, bf16[8,80,128]{2,1,0:T(8,128)(2,1)S(1)}, u32[]{:S(2)}, u32[]{:S(2)}) collective-permute-start(bf16[8,80,128]{2,1,0:T(8,128)(2,1)S(1)} %all_to_all.20.mine), channel_id=1, source_target_pairs={{0,1},{1,0},{2,3},{3,2},{4,5},{5,4},{6,7},{7,6},{8,9},{9,8},{10,11... | collective-permute-start | bytes 491528 | tf_op jit(solution)/shard_map/ppermute | solution.py:434
  45.9 12.5 %copy-start.1 = (bf16[256,5120]{1,0:T(8,128)(2,1)S(1)}, bf16[256,5120]{1,0:T(8,128)(2,1)}, u32[]{:S(2)}) copy-start(bf16[256,5120]{1,0:T(8,128)(2,1)} %o_in.3) | copy-start | bytes 7864324
  48.4 1.5 %collective-permute-start.3 = (bf16[8,80,128]{2,1,0:T(8,128)(2,1)S(1)}, bf16[8,80,128]{2,1,0:T(8,128)(2,1)S(1)}, u32[]{:S(2)}, u32[]{:S(2)}) collective-permute-start(bf16[8,80,128]{2,1,0:T(8,128)(2,1)S(1)} %get-tuple-element.17), channel_id=1, source_target_pairs={{0,1},{1,0},{2,3},{3,2},{4,5},{5,4},{6,7},{7,6},{8,9},{9,8},{10,11... | collective-permute-start | bytes 491528 | tf_op jit(solution)/shard_map/ppermute | solution.py:447
  59.1 2.7 %collective-permute-start.4 = (bf16[8,32,384]{2,1,0:T(8,128)(2,1)S(1)}, bf16[8,32,384]{2,1,0:T(8,128)(2,1)S(1)}, u32[]{:S(2)}, u32[]{:S(2)}) collective-permute-start(bf16[8,32,384]{2,1,0:T(8,128)(2,1)S(1)} %get-tuple-element.23), channel_id=1, source_target_pairs={{0,1},{1,0},{2,3},{3,2},{4,5},{5,4},{6,7},{7,6},{8,9},{9,8},{10,11... | collective-permute-start | bytes 589832 | tf_op jit(solution)/shard_map/ppermute | solution.py:464
where the time goes:
time: 71.2 us; the launch traced here: 70.8 us
  blocking collectives  26.2 us (37%)
  starting transfers between devices  18.6 us (26%)
  waiting for transfers between devices  14.9 us (21%)
  Pallas kernels  8.08 us (11%)
  matrix products  1.93 us (3%)
  local copies, waits for them, and re-layouts  1.08 us (2%)
    all_to_all x1, waiting for transfers between devices, per_device(): factors = lax.all_to_all(message, 'group', 0, 0)  11.8 us
    all_to_all x1, starting transfers between devices, per_device(): factors = lax.all_to_all(message, 'group', 0, 0)  11.6 us
    all_to_all x1, blocking collectives, per_device(): mine = lax.all_to_all(message, 'tp', 0, 0, axis_index_groups=same_core)  9.76 us
    all_to_all x1, blocking collectives, per_device(): sums = lax.all_to_all(message, 'tp', 0, 0, axis_index_groups=same_core)  8.28 us
    all_to_all x1, blocking collectives, per_device(): parts = lax.all_to_all(message, 'tp', 0, 0, axis_index_groups=same_core)  8.14 us
    ppermute x1, starting transfers between devices, per_device(): low_other = lax.ppermute(low_own, 'tp', other_core)  2.32 us
    pallas_call x1, Pallas kernels, per_device(): call(pack_factors, [HBM] * 4, shape(GROUPS, FACTOR_ROWS, HD), [pltpu.VMEM...  1.99 us
    pallas_call x1, Pallas kernels, per_device(): call(cached_attention, [SMEM, VMEM, VMEM, VMEM], [shape(CHIPS, PART_ROWS,...  1.82 us
  transfers between devices with their start and end apart: 6, of which 6 were waited for; matrix products, arithmetic and copies ran while one was open for 4% of the time, Pallas kernels for 2%

commit v1 on v0

--- a/solution.py
+++ b/solution.py
@@ -147,14 +147,14 @@
 
 
 def cached_attention(
-    lengths, mine, theirs, cache, own_part, other_part, queries, weighted, scores, weights
+    gains, mine, theirs, cache, own_part, other_part, queries, weighted, scores, weights
 ):
     first = lax.axis_index("tp") * SLOTS
     core = lax.axis_index("tp") % 2
     for i in range(CHIPS):
         queries[2 * i + core] = mine[i, 0:64, :].astype(F32)
         queries[2 * i + 1 - core] = theirs[i, 0:64, :].astype(F32)
-    position = lanes((HD, SLOTS)) + first
+    position = (lanes((HD, SLOTS)) + first).astype(F32)
     lane = lanes((HD, HD))
     for s in range(SEQS):
         query = queries[:, PER_SEQ * s : PER_SEQ * s + PER_SEQ, :].reshape(HD, HD).astype(BF16)
@@ -168,7 +168,8 @@
     logs = jnp.zeros((HD, HD), F32)
     inverse = []
     for s in range(SEQS):
-        score = jnp.where(position < lengths[0, s], scores[s] * INV_ROOT, FAR)
+        bound = jnp.concatenate([gains[2 + s : 3 + s, :]] * 2, axis=1)
+        score = jnp.where(position < bound, scores[s] * INV_ROOT, FAR)
         largest = score.max(axis=-1, keepdims=True)
         weight = jnp.exp(score - largest)
         total = weight.sum(axis=-1, keepdims=True)
@@ -403,7 +404,8 @@
     query_part = jnp.dot(tokens, q_weight, preferred_element_type=F32)
     keyval_part = jnp.dot(tokens, kv_weight, preferred_element_type=F32)
 
-    gains = jnp.concatenate([q_gain, k_gain], axis=0)
+    bounds = jnp.broadcast_to(lengths.reshape(SEQS, 1).astype(F32), (SEQS, HD))
+    gains = jnp.concatenate([q_gain, k_gain, bounds], axis=0)
     kv_other = lax.ppermute(keyval_part, "tp", other_core)
     low_own = call(
         low_rank,
@@ -435,7 +437,7 @@
 
     own_part, other_part = call(
         cached_attention,
-        [SMEM, VMEM, VMEM, VMEM],
+        [VMEM] * 4,
         [shape(CHIPS, PART_ROWS, HD, dtype=F32), shape(CHIPS, PART_ROWS, HD)],
         [
             pltpu.VMEM((TP, 64, HD), F32),
@@ -443,7 +445,7 @@
             pltpu.VMEM((SEQS, HD, SLOTS), F32),
             pltpu.VMEM((SEQS, HD, SLOTS), BF16),
         ],
-    )(lengths, mine, theirs, cache)
+    )(gains, mine, theirs, cache)
     other_part = lax.ppermute(other_part, "tp", other_core)
     fresh, fresh_logs = call(
         fresh_attention,

time: 71.2 us -> 70.6 us (level)
  no operation moved by 1% of the time
where the time goes in v1:
time: 70.6 us; the launch traced here: 70.3 us
  blocking collectives  26.2 us (37%)
  starting transfers between devices  18.6 us (26%)
  waiting for transfers between devices  14.7 us (21%)
  Pallas kernels  7.48 us (11%)
  matrix products  1.94 us (3%)
  local copies, waits for them, and re-layouts  1.16 us (2%)
    all_to_all x1, waiting for transfers between devices, per_device(): factors = lax.all_to_all(message, 'group', 0, 0)  11.8 us
    all_to_all x1, starting transfers between devices, per_device(): factors = lax.all_to_all(message, 'group', 0, 0)  11.6 us
    all_to_all x1, blocking collectives, per_device(): mine = lax.all_to_all(message, 'tp', 0, 0, axis_index_groups=same_core)  9.76 us
    all_to_all x1, blocking collectives, per_device(): sums = lax.all_to_all(message, 'tp', 0, 0, axis_index_groups=same_core)  8.27 us
    all_to_all x1, blocking collectives, per_device(): parts = lax.all_to_all(message, 'tp', 0, 0, axis_index_groups=same_core)  8.15 us
    ppermute x1, starting transfers between devices, per_device(): low_other = lax.ppermute(low_own, 'tp', other_core)  2.33 us
    pallas_call x1, Pallas kernels, per_device(): call(pack_factors, [HBM] * 4, shape(GROUPS, FACTOR_ROWS, HD), [pltpu.VMEM...  1.99 us
    ppermute x1, starting transfers between devices, per_device(): theirs = lax.ppermute(mine, 'tp', other_core)  1.64 us
  transfers between devices with their start and end apart: 6, of which 6 were waited for; matrix products, arithmetic and copies ran while one was open for 4% of the time, Pallas kernels for 2%

profile of v1, /device:TPU:1, one launch (start us, length us, event | category | flops | bytes accessed | tf_op | source)
XLA Modules:
  0.0 70.3 jit_solution(665199750235383009)
XLA Ops:
  0.0 2.0 %shard_map.127 = bf16[16,112,128]{2,1,0:T(8,128)(2,1)} custom-call(bf16[64,320]{1,0:T(8,128)(2,1)} %bitcast.10, bf16[4,256]{1,0:T(4,128)(2,1)} %b_q.1, bf16[4,256]{1,0:T(4,128)(2,1)} %bitcast.11, bf16[4,320]{1,0:T(4,128)(2,1)} %b_o.1), custom_call_target="tpu_custom_call" | custom-call | flops 1000000 | bytes 1000000 | tf_op jit(solution)/shard_map/pallas_call | solution.py:387
  2.0 11.6 %all-to-all-start = ((bf16[16,112,128]{2,1,0:T(8,128)(2,1)}), bf16[16,112,128]{2,1,0:T(8,128)(2,1)S(1)}, u32[]{:S(2)}, u32[]{:S(2)}) async-start(bf16[16,112,128]{2,1,0:T(8,128)(2,1)} %shard_map.127), calls=%async_computation | async-start | bytes 917504 | tf_op jit(solution)/shard_map/all_to_all | solution.py:402
  13.6 1.1 %reshape.20.tokens = bf16[32,5120]{1,0:T(8,128)(2,1)S(1)} reshape(bf16[1,8,4,5120]{3,2,1,0:T(4,128)(2,1)} %param.13) | data formatting | bytes 655360 | tf_op jit(solution)/shard_map/reshape | solution.py:382
  14.7 1.4 %fusion.1.kv_own = f32[32,64]{1,0:T(8,128)S(1)} fusion(bf16[32,5120]{1,0:T(8,128)(2,1)S(1)} %reshape.20.tokens, bf16[5120,64]{0,1:T(8,128)(2,1)} %param.15), kind=kOutput, calls=%fused_computation.3 | convolution fusion | flops 20971520 | bytes 991232 | tf_op jit(solution)/shard_map/dot_general | solution.py:405
  16.1 1.0 %collective-permute-start = (f32[32,64]{1,0:T(8,128)S(1)}, f32[32,64]{1,0:T(8,128)S(1)}, u32[]{:S(2)}, u32[]{:S(2)}) collective-permute-start(f32[32,64]{1,0:T(8,128)S(1)} %fusion.1.kv_own), channel_id=1, source_target_pairs={{0,1},{1,0},{2,3},{3,2},{4,5},{5,4},{6,7},{7,6},{8,9},{9,8},{10,11... | collective-permute-start | bytes 24584 | tf_op jit(solution)/shard_map/ppermute | solution.py:409
  17.0 0.1 pad.2.clone
  17.1 0.1 maximum_maximum_fusion.__.gains
  17.2 0.7 collective-permute-done._.kv_other
  17.9 11.8 %all-to-all-done.factors = bf16[16,112,128]{2,1,0:T(8,128)(2,1)S(1)} async-done(((bf16[16,112,128]{2,1,0:T(8,128)(2,1)}), bf16[16,112,128]{2,1,0:T(8,128)(2,1)S(1)}, u32[]{:S(2)}, u32[]{:S(2)}) %all-to-all-start) | async-done | bytes 458784 | tf_op jit(solution)/shard_map/all_to_all | solution.py:402
  29.7 1.1 %shard_map.128.low_own = f32[32,128]{1,0:T(8,128)S(1)} custom-call(s32[16]{0:T(128)S(1)} %copy-done.3, bf16[32,5120]{1,0:T(8,128)(2,1)S(1)} %reshape.20.tokens, bf16[16,112,128]{2,1,0:T(8,128)(2,1)S(1)} %all-to-all-done.factors, f32[32,64]{1,0:T(8,128)S(1)} %collective-permute-done._.kv_other, f32[10,128]{1,0:T(8,128)S(1)} %maximum_maximum_fusion.__.gains), custom_call_target="tpu_custom_call" | custom-call | flops 1000000 | bytes 1000000 | tf_op jit(solution)/shard_map/pallas_call | solution.py:410
  30.7 2.3 %collective-permute-start.1 = (f32[32,128]{1,0:T(8,128)S(1)}, f32[32,128]{1,0:T(8,128)S(1)}, u32[]{:S(2)}, u32[]{:S(2)}) collective-permute-start(f32[32,128]{1,0:T(8,128)S(1)} %shard_map.128.low_own), channel_id=1, source_target_pairs={{0,1},{1,0},{2,3},{3,2},{4,5},{5,4},{6,7},{7,6},{8,9},{9,8},{10,11... | collective-permute-start | bytes 49160 | tf_op jit(solution)/shard_map/ppermute | solution.py:416
  33.1 0.6 fusion.query_part
  33.6 0.1 shard_map.129
  33.7 0.2 collective-permute-done.1.low_other
  33.9 0.2 shard_map.130._
  34.1 9.8 %all_to_all.20.mine = bf16[8,80,128]{2,1,0:T(8,128)(2,1)S(1)} all-to-all(bf16[8,80,128]{2,1,0:T(8,128)(2,1)S(1)} %shard_map.130._), channel_id=1, replica_groups={{0,2,4,6,8,10,12,14},{1,3,5,7,9,11,13,15},{16,18,20,22,24,26,28,30},{17..., dimensions={0} | all-to-all | bytes 327680 | tf_op jit(solution)/shard_map/all_to_all | solution.py:429
  43.9 1.6 %collective-permute-start.2 = (bf16[8,80,128]{2,1,0:T(8,128)(2,1)S(1)}, bf16[8,80,128]{2,1,0:T(8,128)(2,1)S(1)}, u32[]{:S(2)}, u32[]{:S(2)}) collective-permute-start(bf16[8,80,128]{2,1,0:T(8,128)(2,1)S(1)} %all_to_all.20.mine), channel_id=1, source_target_pairs={{0,1},{1,0},{2,3},{3,2},{4,5},{5,4},{6,7},{7,6},{8,9},{9,8},{10,11... | collective-permute-start | bytes 491528 | tf_op jit(solution)/shard_map/ppermute | solution.py:436
  45.5 0.4 shard_map.131.cache
  45.9 0.0 copy-start.1
  45.9 0.6 collective-permute-done.2.theirs
  46.6 1.2 %shard_map.132 = (f32[8,80,128]{2,1,0:T(8,128)S(1)}, bf16[8,80,128]{2,1,0:T(8,128)(2,1)S(1)}) custom-call(f32[10,128]{1,0:T(8,128)S(1)} %maximum_maximum_fusion.__.gains, bf16[8,80,128]{2,1,0:T(8,128)(2,1)S(1)} %all_to_all.20.mine, bf16[8,80,128]{2,1,0:T(8,128)(2,1)S(1)} %collective-permute-done.2.theirs, bf16[1,8,2,4,256,128]{5,4,3,2,1,0:T(8,128)(2,1)S(1)} %shard_map.131.cache), custom_call_target="tpu_custom_call" | custom-call | flops 1000000 | bytes 1000000 | tf_op jit(solution)/shard_map/pallas_call | solution.py:438
  47.8 0.5 collective-permute-start.3
  48.2 0.3 shard_map.133
  48.6 0.7 collective-permute-done.3.other
  49.3 0.4 shard_map.134
  49.7 8.1 %all_to_all.21.received = bf16[8,80,128]{2,1,0:T(8,128)(2,1)S(1)} all-to-all(bf16[8,80,128]{2,1,0:T(8,128)(2,1)S(1)} %shard_map.134), channel_id=1, replica_groups={{0,2,4,6,8,10,12,14},{1,3,5,7,9,11,13,15},{16,18,20,22,24,26,28,30},{17..., dimensions={0} | all-to-all | bytes 327680 | tf_op jit(solution)/shard_map/all_to_all | solution.py:459
  57.8 0.7 shard_map.135
  58.5 1.6 %collective-permute-start.4 = (bf16[8,32,384]{2,1,0:T(8,128)(2,1)S(1)}, bf16[8,32,384]{2,1,0:T(8,128)(2,1)S(1)}, u32[]{:S(2)}, u32[]{:S(2)}) collective-permute-start(bf16[8,32,384]{2,1,0:T(8,128)(2,1)S(1)} %get-tuple-element.23), channel_id=1, source_target_pairs={{0,1},{1,0},{2,3},{3,2},{4,5},{5,4},{6,7},{7,6},{8,9},{9,8},{10,11... | collective-permute-start | bytes 589832 | tf_op jit(solution)/shard_map/ppermute | solution.py:466
  60.1 0.3 shard_map.136.mine
  60.4 0.7 %collective-permute-done.4.theirs = bf16[8,32,384]{2,1,0:T(8,128)(2,1)S(1)} collective-permute-done((bf16[8,32,384]{2,1,0:T(8,128)(2,1)S(1)}, bf16[8,32,384]{2,1,0:T(8,128)(2,1)S(1)}, u32[]{:S(2)}, u32[]{:S(2)}) %collective-permute-start.4) | collective-permute-done | bytes 196640 | tf_op jit(solution)/shard_map/ppermute | solution.py:466
  61.2 8.3 %all_to_all.22.received = bf16[8,32,384]{2,1,0:T(8,128)(2,1)S(1)} all-to-all(bf16[8,32,384]{2,1,0:T(8,128)(2,1)S(1)} %shard_map.137), channel_id=1, replica_groups={{0,2,4,6,8,10,12,14},{1,3,5,7,9,11,13,15},{16,18,20,22,24,26,28,30},{17..., dimensions={0} | all-to-all | bytes 393216 | tf_op jit(solution)/shard_map/all_to_all | solution.py:473
  69.5 0.8 %shard_map.138 = bf16[1,8,4,320]{3,2,1,0:T(4,128)(2,1)} custom-call(bf16[8,32,384]{2,1,0:T(8,128)(2,1)S(1)} %all_to_all.22.received, bf16[128,384]{1,0:T(8,128)(2,1)S(1)} %get-tuple-element.24.bo), custom_call_target="tpu_custom_call" | custom-call | flops 1000000 | bytes 1000000 | tf_op jit(solution)/shard_map/pallas_call | solution.py:474
  (15 shorter events, 0.1 us)
Async XLA Ops:
  0.0 33.1 %copy-start = (bf16[5120,256]{1,0:T(8,128)(2,1)S(1)}, bf16[5120,256]{1,0:T(8,128)(2,1)}, u32[]{:S(2)}) copy-start(bf16[5120,256]{1,0:T(8,128)(2,1)} %param.14) | copy-start | bytes 7864324
  0.0 17.0 %copy-start.6 = (s32[1,8]{1,0:T(1,128)S(1)}, s32[1,8]{1,0:T(1,128)}, u32[]{:S(2)}) copy-start(s32[1,8]{1,0:T(1,128)} %param.20) | copy-start | bytes 100
  0.0 17.1 %copy-start.5 = (f32[128]{0:T(128)S(1)}, f32[128]{0:T(128)}, u32[]{:S(2)}) copy-start(f32[128]{0:T(128)} %param.17) | copy-start | bytes 1540
  0.0 17.1 %copy-start.4 = (f32[128]{0:T(128)S(1)}, f32[128]{0:T(128)}, u32[]{:S(2)}) copy-start(f32[128]{0:T(128)} %param.18) | copy-start | bytes 1540
  0.0 29.6 %copy-start.3 = (s32[16]{0:T(128)S(1)}, s32[16]{0:T(128)}, u32[]{:S(2)}) copy-start(s32[16]{0:T(128)} %owner.1) | copy-start | bytes 196
  2.0 27.6 %all-to-all-start = ((bf16[16,112,128]{2,1,0:T(8,128)(2,1)}), bf16[16,112,128]{2,1,0:T(8,128)(2,1)S(1)}, u32[]{:S(2)}, u32[]{:S(2)}) async-start(bf16[16,112,128]{2,1,0:T(8,128)(2,1)} %shard_map.127), calls=%async_computation | async-start | bytes 917504 | tf_op jit(solution)/shard_map/all_to_all | solution.py:402
  16.1 1.8 %collective-permute-start = (f32[32,64]{1,0:T(8,128)S(1)}, f32[32,64]{1,0:T(8,128)S(1)}, u32[]{:S(2)}, u32[]{:S(2)}) collective-permute-start(f32[32,64]{1,0:T(8,128)S(1)} %fusion.1.kv_own), channel_id=1, source_target_pairs={{0,1},{1,0},{2,3},{3,2},{4,5},{5,4},{6,7},{7,6},{8,9},{9,8},{10,11... | collective-permute-start | bytes 24584 | tf_op jit(solution)/shard_map/ppermute | solution.py:409
  29.7 15.9 %copy-start.2 = (bf16[1,8,2,4,256,128]{5,4,3,2,1,0:T(8,128)(2,1)S(1)}, bf16[1,8,2,4,256,128]{5,4,3,2,1,0:T(8,128)(2,1)}, u32[]{:S(2)}) copy-start(bf16[1,8,2,4,256,128]{5,4,3,2,1,0:T(8,128)(2,1)} %cache.1) | copy-start | bytes 12582916
  30.7 3.2 %collective-permute-start.1 = (f32[32,128]{1,0:T(8,128)S(1)}, f32[32,128]{1,0:T(8,128)S(1)}, u32[]{:S(2)}, u32[]{:S(2)}) collective-permute-start(f32[32,128]{1,0:T(8,128)S(1)} %shard_map.128.low_own), channel_id=1, source_target_pairs={{0,1},{1,0},{2,3},{3,2},{4,5},{5,4},{6,7},{7,6},{8,9},{9,8},{10,11... | collective-permute-start | bytes 49160 | tf_op jit(solution)/shard_map/ppermute | solution.py:416
  43.9 2.7 %collective-permute-start.2 = (bf16[8,80,128]{2,1,0:T(8,128)(2,1)S(1)}, bf16[8,80,128]{2,1,0:T(8,128)(2,1)S(1)}, u32[]{:S(2)}, u32[]{:S(2)}) collective-permute-start(bf16[8,80,128]{2,1,0:T(8,128)(2,1)S(1)} %all_to_all.20.mine), channel_id=1, source_target_pairs={{0,1},{1,0},{2,3},{3,2},{4,5},{5,4},{6,7},{7,6},{8,9},{9,8},{10,11... | collective-permute-start | bytes 491528 | tf_op jit(solution)/shard_map/ppermute | solution.py:436
  45.9 11.9 %copy-start.1 = (bf16[256,5120]{1,0:T(8,128)(2,1)S(1)}, bf16[256,5120]{1,0:T(8,128)(2,1)}, u32[]{:S(2)}) copy-start(bf16[256,5120]{1,0:T(8,128)(2,1)} %o_in.3) | copy-start | bytes 7864324
  47.8 1.5 %collective-permute-start.3 = (bf16[8,80,128]{2,1,0:T(8,128)(2,1)S(1)}, bf16[8,80,128]{2,1,0:T(8,128)(2,1)S(1)}, u32[]{:S(2)}, u32[]{:S(2)}) collective-permute-start(bf16[8,80,128]{2,1,0:T(8,128)(2,1)S(1)} %get-tuple-element.17), channel_id=1, source_target_pairs={{0,1},{1,0},{2,3},{3,2},{4,5},{5,4},{6,7},{7,6},{8,9},{9,8},{10,11... | collective-permute-start | bytes 491528 | tf_op jit(solution)/shard_map/ppermute | solution.py:449
  58.5 2.7 %collective-permute-start.4 = (bf16[8,32,384]{2,1,0:T(8,128)(2,1)S(1)}, bf16[8,32,384]{2,1,0:T(8,128)(2,1)S(1)}, u32[]{:S(2)}, u32[]{:S(2)}) collective-permute-start(bf16[8,32,384]{2,1,0:T(8,128)(2,1)S(1)} %get-tuple-element.23), channel_id=1, source_target_pairs={{0,1},{1,0},{2,3},{3,2},{4,5},{5,4},{6,7},{7,6},{8,9},{9,8},{10,11... | collective-permute-start | bytes 589832 | tf_op jit(solution)/shard_map/ppermute | solution.py:466

commit v2 on v1

--- a/solution.py
+++ b/solution.py
@@ -101,7 +101,7 @@
     right = jnp.where(lane < R, 0.0, 1.0).astype(BF16)
     empty = jnp.zeros((HALF, HD), BF16)
     for g in range(GROUPS):
-        base = owner[g] * BLOCK
+        base = owner[0, g] * BLOCK
         mine = pl.multiple_of(base + core * HALF, 32)
         other = pl.multiple_of(base + (1 - core) * HALF, 32)
         block = factors[g, 0:80, :]
@@ -409,10 +409,10 @@
     kv_other = lax.ppermute(keyval_part, "tp", other_core)
     low_own = call(
         low_rank,
-        [SMEM, VMEM, VMEM, VMEM, VMEM],
+        [VMEM] * 5,
         shape(ROWS, HD, dtype=F32),
         [pltpu.VMEM((WIDTH, HD), BF16)],
-    )(owner, tokens, factors, kv_other, gains)
+    )(owner.reshape(1, GROUPS), tokens, factors, kv_other, gains)
     low_other = lax.ppermute(low_own, "tp", other_core)
     bq, ao, bo = call(
         unpack_factors,

time: 70.6 us -> 70.2 us (level)
  no operation moved by 1% of the time
where the time goes in v2:
time: 70.2 us; the launch traced here: 69.8 us
  blocking collectives  26.2 us (37%)
  starting transfers between devices  18.6 us (26%)
  waiting for transfers between devices  14.7 us (21%)
  Pallas kernels  7.02 us (10%)
  matrix products  1.94 us (3%)
  local copies, waits for them, and re-layouts  1.16 us (2%)
    all_to_all x1, waiting for transfers between devices, per_device(): factors = lax.all_to_all(message, 'group', 0, 0)  11.8 us
    all_to_all x1, starting transfers between devices, per_device(): factors = lax.all_to_all(message, 'group', 0, 0)  11.6 us
    all_to_all x1, blocking collectives, per_device(): mine = lax.all_to_all(message, 'tp', 0, 0, axis_index_groups=same_core)  9.76 us
    all_to_all x1, blocking collectives, per_device(): sums = lax.all_to_all(message, 'tp', 0, 0, axis_index_groups=same_core)  8.28 us
    all_to_all x1, blocking collectives, per_device(): parts = lax.all_to_all(message, 'tp', 0, 0, axis_index_groups=same_core)  8.14 us
    ppermute x1, starting transfers between devices, per_device(): low_other = lax.ppermute(low_own, 'tp', other_core)  2.32 us
    pallas_call x1, Pallas kernels, per_device(): call(pack_factors, [HBM] * 4, shape(GROUPS, FACTOR_ROWS, HD), [pltpu.VMEM...  1.99 us
    ppermute x1, starting transfers between devices, per_device(): theirs = lax.ppermute(mine, 'tp', other_core)  1.64 us
  transfers between devices with their start and end apart: 6, of which 6 were waited for; matrix products, arithmetic and copies ran while one was open for 4% of the time, Pallas kernels for 2%

profile of v2, /device:TPU:1, one launch (start us, length us, event | category | flops | bytes accessed | tf_op | source)
XLA Modules:
  0.0 69.8 jit_solution(4711255385774197057)
XLA Ops:
  0.0 2.0 %shard_map.127 = bf16[16,112,128]{2,1,0:T(8,128)(2,1)} custom-call(bf16[64,320]{1,0:T(8,128)(2,1)} %bitcast.12, bf16[4,256]{1,0:T(4,128)(2,1)} %b_q.1, bf16[4,256]{1,0:T(4,128)(2,1)} %bitcast.13, bf16[4,320]{1,0:T(4,128)(2,1)} %b_o.1), custom_call_target="tpu_custom_call" | custom-call | flops 1000000 | bytes 1000000 | tf_op jit(solution)/shard_map/pallas_call | solution.py:387
  2.0 11.6 %all-to-all-start = ((bf16[16,112,128]{2,1,0:T(8,128)(2,1)}), bf16[16,112,128]{2,1,0:T(8,128)(2,1)S(1)}, u32[]{:S(2)}, u32[]{:S(2)}) async-start(bf16[16,112,128]{2,1,0:T(8,128)(2,1)} %shard_map.127), calls=%async_computation | async-start | bytes 917504 | tf_op jit(solution)/shard_map/all_to_all | solution.py:402
  13.6 1.1 %reshape.23.tokens = bf16[32,5120]{1,0:T(8,128)(2,1)S(1)} reshape(bf16[1,8,4,5120]{3,2,1,0:T(4,128)(2,1)} %param.13) | data formatting | bytes 655360 | tf_op jit(solution)/shard_map/reshape | solution.py:382
  14.7 1.4 %fusion.1.kv_own = f32[32,64]{1,0:T(8,128)S(1)} fusion(bf16[32,5120]{1,0:T(8,128)(2,1)S(1)} %reshape.23.tokens, bf16[5120,64]{0,1:T(8,128)(2,1)} %param.15), kind=kOutput, calls=%fused_computation.3 | convolution fusion | flops 20971520 | bytes 991232 | tf_op jit(solution)/shard_map/dot_general | solution.py:405
  16.1 1.0 %collective-permute-start = (f32[32,64]{1,0:T(8,128)S(1)}, f32[32,64]{1,0:T(8,128)S(1)}, u32[]{:S(2)}, u32[]{:S(2)}) collective-permute-start(f32[32,64]{1,0:T(8,128)S(1)} %fusion.1.kv_own), channel_id=1, source_target_pairs={{0,1},{1,0},{2,3},{3,2},{4,5},{5,4},{6,7},{7,6},{8,9},{9,8},{10,11... | collective-permute-start | bytes 24584 | tf_op jit(solution)/shard_map/ppermute | solution.py:409
  17.0 0.1 pad.2.clone
  17.1 0.1 maximum_maximum_fusion.__.gains
  17.2 0.7 collective-permute-done._.kv_other
  17.9 11.8 %all-to-all-done.factors = bf16[16,112,128]{2,1,0:T(8,128)(2,1)S(1)} async-done(((bf16[16,112,128]{2,1,0:T(8,128)(2,1)}), bf16[16,112,128]{2,1,0:T(8,128)(2,1)S(1)}, u32[]{:S(2)}, u32[]{:S(2)}) %all-to-all-start) | async-done | bytes 458784 | tf_op jit(solution)/shard_map/all_to_all | solution.py:402
  29.7 0.6 shard_map.128.low_own
  30.3 2.3 %collective-permute-start.1 = (f32[32,128]{1,0:T(8,128)S(1)}, f32[32,128]{1,0:T(8,128)S(1)}, u32[]{:S(2)}, u32[]{:S(2)}) collective-permute-start(f32[32,128]{1,0:T(8,128)S(1)} %shard_map.128.low_own), channel_id=1, source_target_pairs={{0,1},{1,0},{2,3},{3,2},{4,5},{5,4},{6,7},{7,6},{8,9},{9,8},{10,11... | collective-permute-start | bytes 49160 | tf_op jit(solution)/shard_map/ppermute | solution.py:416
  32.6 0.6 fusion.query_part
  33.1 0.1 shard_map.129
  33.2 0.2 collective-permute-done.1.low_other
  33.4 0.2 shard_map.130._
  33.7 9.8 %all_to_all.20.mine = bf16[8,80,128]{2,1,0:T(8,128)(2,1)S(1)} all-to-all(bf16[8,80,128]{2,1,0:T(8,128)(2,1)S(1)} %shard_map.130._), channel_id=1, replica_groups={{0,2,4,6,8,10,12,14},{1,3,5,7,9,11,13,15},{16,18,20,22,24,26,28,30},{17..., dimensions={0} | all-to-all | bytes 327680 | tf_op jit(solution)/shard_map/all_to_all | solution.py:429
  43.4 1.6 %collective-permute-start.2 = (bf16[8,80,128]{2,1,0:T(8,128)(2,1)S(1)}, bf16[8,80,128]{2,1,0:T(8,128)(2,1)S(1)}, u32[]{:S(2)}, u32[]{:S(2)}) collective-permute-start(bf16[8,80,128]{2,1,0:T(8,128)(2,1)S(1)} %all_to_all.20.mine), channel_id=1, source_target_pairs={{0,1},{1,0},{2,3},{3,2},{4,5},{5,4},{6,7},{7,6},{8,9},{9,8},{10,11... | collective-permute-start | bytes 491528 | tf_op jit(solution)/shard_map/ppermute | solution.py:436
  45.1 0.4 shard_map.131.cache
  45.5 0.0 copy-start.1
  45.5 0.6 collective-permute-done.2.theirs
  46.1 1.2 %shard_map.132 = (f32[8,80,128]{2,1,0:T(8,128)S(1)}, bf16[8,80,128]{2,1,0:T(8,128)(2,1)S(1)}) custom-call(f32[10,128]{1,0:T(8,128)S(1)} %maximum_maximum_fusion.__.gains, bf16[8,80,128]{2,1,0:T(8,128)(2,1)S(1)} %all_to_all.20.mine, bf16[8,80,128]{2,1,0:T(8,128)(2,1)S(1)} %collective-permute-done.2.theirs, bf16[1,8,2,4,256,128]{5,4,3,2,1,0:T(8,128)(2,1)S(1)} %shard_map.131.cache), custom_call_target="tpu_custom_call" | custom-call | flops 1000000 | bytes 1000000 | tf_op jit(solution)/shard_map/pallas_call | solution.py:438
  47.3 0.5 collective-permute-start.3
  47.8 0.3 shard_map.133
  48.1 0.7 collective-permute-done.3.other
  48.8 0.4 shard_map.134
  49.2 8.1 %all_to_all.21.received = bf16[8,80,128]{2,1,0:T(8,128)(2,1)S(1)} all-to-all(bf16[8,80,128]{2,1,0:T(8,128)(2,1)S(1)} %shard_map.134), channel_id=1, replica_groups={{0,2,4,6,8,10,12,14},{1,3,5,7,9,11,13,15},{16,18,20,22,24,26,28,30},{17..., dimensions={0} | all-to-all | bytes 327680 | tf_op jit(solution)/shard_map/all_to_all | solution.py:459
  57.3 0.7 shard_map.135
  58.0 1.6 %collective-permute-start.4 = (bf16[8,32,384]{2,1,0:T(8,128)(2,1)S(1)}, bf16[8,32,384]{2,1,0:T(8,128)(2,1)S(1)}, u32[]{:S(2)}, u32[]{:S(2)}) collective-permute-start(bf16[8,32,384]{2,1,0:T(8,128)(2,1)S(1)} %get-tuple-element.23), channel_id=1, source_target_pairs={{0,1},{1,0},{2,3},{3,2},{4,5},{5,4},{6,7},{7,6},{8,9},{9,8},{10,11... | collective-permute-start | bytes 589832 | tf_op jit(solution)/shard_map/ppermute | solution.py:466
  59.6 0.3 shard_map.136.mine
  60.0 0.7 %collective-permute-done.4.theirs = bf16[8,32,384]{2,1,0:T(8,128)(2,1)S(1)} collective-permute-done((bf16[8,32,384]{2,1,0:T(8,128)(2,1)S(1)}, bf16[8,32,384]{2,1,0:T(8,128)(2,1)S(1)}, u32[]{:S(2)}, u32[]{:S(2)}) %collective-permute-start.4) | collective-permute-done | bytes 196640 | tf_op jit(solution)/shard_map/ppermute | solution.py:466
  60.7 8.3 %all_to_all.22.received = bf16[8,32,384]{2,1,0:T(8,128)(2,1)S(1)} all-to-all(bf16[8,32,384]{2,1,0:T(8,128)(2,1)S(1)} %shard_map.137), channel_id=1, replica_groups={{0,2,4,6,8,10,12,14},{1,3,5,7,9,11,13,15},{16,18,20,22,24,26,28,30},{17..., dimensions={0} | all-to-all | bytes 393216 | tf_op jit(solution)/shard_map/all_to_all | solution.py:473
  69.0 0.8 %shard_map.138 = bf16[1,8,4,320]{3,2,1,0:T(4,128)(2,1)} custom-call(bf16[8,32,384]{2,1,0:T(8,128)(2,1)S(1)} %all_to_all.22.received, bf16[128,384]{1,0:T(8,128)(2,1)S(1)} %get-tuple-element.24.bo), custom_call_target="tpu_custom_call" | custom-call | flops 1000000 | bytes 1000000 | tf_op jit(solution)/shard_map/pallas_call | solution.py:474
  (15 shorter events, 0.1 us)
Async XLA Ops:
  0.0 32.6 %copy-start = (bf16[5120,256]{1,0:T(8,128)(2,1)S(1)}, bf16[5120,256]{1,0:T(8,128)(2,1)}, u32[]{:S(2)}) copy-start(bf16[5120,256]{1,0:T(8,128)(2,1)} %param.14) | copy-start | bytes 7864324
  0.0 17.0 %copy-start.6 = (s32[1,8]{1,0:T(1,128)S(1)}, s32[1,8]{1,0:T(1,128)}, u32[]{:S(2)}) copy-start(s32[1,8]{1,0:T(1,128)} %param.20) | copy-start | bytes 100
  0.0 17.1 %copy-start.5 = (f32[128]{0:T(128)S(1)}, f32[128]{0:T(128)}, u32[]{:S(2)}) copy-start(f32[128]{0:T(128)} %param.17) | copy-start | bytes 1540
  0.0 17.1 %copy-start.4 = (f32[128]{0:T(128)S(1)}, f32[128]{0:T(128)}, u32[]{:S(2)}) copy-start(f32[128]{0:T(128)} %param.18) | copy-start | bytes 1540
  0.0 29.6 %copy-start.3 = (s32[16]{0:T(128)S(1)}, s32[16]{0:T(128)}, u32[]{:S(2)}) copy-start(s32[16]{0:T(128)} %param.21) | copy-start | bytes 196
  2.0 27.6 %all-to-all-start = ((bf16[16,112,128]{2,1,0:T(8,128)(2,1)}), bf16[16,112,128]{2,1,0:T(8,128)(2,1)S(1)}, u32[]{:S(2)}, u32[]{:S(2)}) async-start(bf16[16,112,128]{2,1,0:T(8,128)(2,1)} %shard_map.127), calls=%async_computation | async-start | bytes 917504 | tf_op jit(solution)/shard_map/all_to_all | solution.py:402
  16.1 1.8 %collective-permute-start = (f32[32,64]{1,0:T(8,128)S(1)}, f32[32,64]{1,0:T(8,128)S(1)}, u32[]{:S(2)}, u32[]{:S(2)}) collective-permute-start(f32[32,64]{1,0:T(8,128)S(1)} %fusion.1.kv_own), channel_id=1, source_target_pairs={{0,1},{1,0},{2,3},{3,2},{4,5},{5,4},{6,7},{7,6},{8,9},{9,8},{10,11... | collective-permute-start | bytes 24584 | tf_op jit(solution)/shard_map/ppermute | solution.py:409
  29.7 15.4 %copy-start.2 = (bf16[1,8,2,4,256,128]{5,4,3,2,1,0:T(8,128)(2,1)S(1)}, bf16[1,8,2,4,256,128]{5,4,3,2,1,0:T(8,128)(2,1)}, u32[]{:S(2)}) copy-start(bf16[1,8,2,4,256,128]{5,4,3,2,1,0:T(8,128)(2,1)} %cache.1) | copy-start | bytes 12582916
  30.3 3.2 %collective-permute-start.1 = (f32[32,128]{1,0:T(8,128)S(1)}, f32[32,128]{1,0:T(8,128)S(1)}, u32[]{:S(2)}, u32[]{:S(2)}) collective-permute-start(f32[32,128]{1,0:T(8,128)S(1)} %shard_map.128.low_own), channel_id=1, source_target_pairs={{0,1},{1,0},{2,3},{3,2},{4,5},{5,4},{6,7},{7,6},{8,9},{9,8},{10,11... | collective-permute-start | bytes 49160 | tf_op jit(solution)/shard_map/ppermute | solution.py:416
  43.4 2.7 %collective-permute-start.2 = (bf16[8,80,128]{2,1,0:T(8,128)(2,1)S(1)}, bf16[8,80,128]{2,1,0:T(8,128)(2,1)S(1)}, u32[]{:S(2)}, u32[]{:S(2)}) collective-permute-start(bf16[8,80,128]{2,1,0:T(8,128)(2,1)S(1)} %all_to_all.20.mine), channel_id=1, source_target_pairs={{0,1},{1,0},{2,3},{3,2},{4,5},{5,4},{6,7},{7,6},{8,9},{9,8},{10,11... | collective-permute-start | bytes 491528 | tf_op jit(solution)/shard_map/ppermute | solution.py:436
  45.5 11.9 %copy-start.1 = (bf16[256,5120]{1,0:T(8,128)(2,1)S(1)}, bf16[256,5120]{1,0:T(8,128)(2,1)}, u32[]{:S(2)}) copy-start(bf16[256,5120]{1,0:T(8,128)(2,1)} %o_in.3) | copy-start | bytes 7864324
  47.3 1.5 %collective-permute-start.3 = (bf16[8,80,128]{2,1,0:T(8,128)(2,1)S(1)}, bf16[8,80,128]{2,1,0:T(8,128)(2,1)S(1)}, u32[]{:S(2)}, u32[]{:S(2)}) collective-permute-start(bf16[8,80,128]{2,1,0:T(8,128)(2,1)S(1)} %get-tuple-element.17), channel_id=1, source_target_pairs={{0,1},{1,0},{2,3},{3,2},{4,5},{5,4},{6,7},{7,6},{8,9},{9,8},{10,11... | collective-permute-start | bytes 491528 | tf_op jit(solution)/shard_map/ppermute | solution.py:449
  58.0 2.7 %collective-permute-start.4 = (bf16[8,32,384]{2,1,0:T(8,128)(2,1)S(1)}, bf16[8,32,384]{2,1,0:T(8,128)(2,1)S(1)}, u32[]{:S(2)}, u32[]{:S(2)}) collective-permute-start(bf16[8,32,384]{2,1,0:T(8,128)(2,1)S(1)} %get-tuple-element.23), channel_id=1, source_target_pairs={{0,1},{1,0},{2,3},{3,2},{4,5},{5,4},{6,7},{7,6},{8,9},{9,8},{10,11... | collective-permute-start | bytes 589832 | tf_op jit(solution)/shard_map/ppermute | solution.py:466
